TPU v7x, 256 devices: a whole 4x4x8 slice. The times are simulated.
256 devices in a mesh: ctx: 16 (over y_hi, x, core), exp: 8 (over z), dp: 2 (over y_lo).
Axes of the slice: x: 4, y: 4 (y_hi: 2, y_lo: 2; y = y_hi * 2 + y_lo), z: 8, core: 2. Of those that a mesh axis runs over, the one named last changes fastest.
Arguments:
- tokens: bfloat16 [2, 2048, 4096], P('dp', 'ctx'), may hold values from -6 to 6
- norm_in: bfloat16 [4096], replicated, may hold values from 0.099609375 to 1.8984375
- w_qkv: bfloat16 [4096, 8, 6, 128], P('dp', 'exp')
- w_out: bfloat16 [8, 4, 128, 4096], P('exp', None, None, 'dp'), may hold values from -0.375 to 0.375
- norm_mid: bfloat16 [4096], replicated, may hold values from 0.099609375 to 1.8984375
- w_router: bfloat16 [4096, 8], replicated, may hold values from -0.09375 to 0.09375
- w_gate_up: bfloat16 [8, 4096, 2, 8192], P('exp', 'dp', None, 'ctx'), may hold values from -0.09375 to 0.09375
- w_down: bfloat16 [8, 8192, 4096], P('exp', 'ctx', 'dp'), may hold values from -0.0625 to 0.0625
- expert_ids: int32 [2, 2048, 2], P('dp', ('ctx', 'exp')), may hold values from 0 to 7, as said below
- slot_index: int32 [2, 2048, 2], P('dp', ('ctx', 'exp')), may hold values from 0 to 5, as said below
Outputs:
- layer_out: bfloat16 [2, 2048, 4096], P('dp', ('ctx', 'exp'))
Inputs may be any that keep to these rules, and one draw needn't show every extreme that they name: `expert_ids`: each token names two different experts; in every aligned block of 16 tokens (the tokens of one device) the numbers of choices of the experts are, in some order, 6, 5, 4, 4, 4, 3, 3 and 3, so that no expert is named more than 6 times and one exactly 6 times. `slot_index`: a choice's slot is the number of earlier choices of the same expert in its block of 16 tokens, a token's first choice counting before its second.
All inputs are finite; a program needn't handle non-finite values.
Results may differ from a plain program's by a relative error of at most 0.022.
The roundings to bfloat16 on the way count: a program that leaves them out, or rounds other values in their place, can miss the bound.
Values may be sent and summed in bfloat16 or wider, within the bound.
No kernel may reach another device: no remote copies, remote signals or barrier semaphores. Data moves between devices by JAX's collectives and lax.ppermute only.
A program may use at most 128 MiB of HBM per device.

v0:
```python
import math
import jax
import jax.numpy as jnp
from jax import lax
from jax.sharding import PartitionSpec as P

EPSILON = 1e-05
ROPE_BASE = 1000000.0


def rms_norm(values, gain):
    wide = values.astype(jnp.float32)
    square_mean = jnp.mean(wide * wide, axis=-1, keepdims=True)
    return (wide * lax.rsqrt(square_mean + EPSILON) * gain.astype(jnp.float32)).astype(jnp.bfloat16)


def rope_angles(positions, head_dim):
    half_dim = head_dim // 2
    freqs = jnp.exp(
        jnp.arange(half_dim, dtype=jnp.float32) * (-2.0 * math.log(ROPE_BASE) / head_dim)
    )
    return positions[:, None] * freqs[None, :]


def rotate(tensor, angles):
    half_dim = tensor.shape[-1] // 2
    first_half = tensor[..., :half_dim]
    second_half = tensor[..., half_dim:]
    cosine = jnp.cos(angles)
    sine = jnp.sin(angles)
    return jnp.concatenate(
        [first_half * cosine - second_half * sine, second_half * cosine + first_half * sine],
        axis=-1,
    )


def on_device(
    tokens, norm_in, w_qkv, w_out, norm_mid, w_router, w_gate_up, w_down, expert_ids, slot_index
):
    tok_rows = tokens.shape[1]
    head_dim = w_qkv.shape[3]
    kv_local = w_qkv.shape[1]
    group_size = w_qkv.shape[2] - 2
    width = tokens.shape[2]
    normed = rms_norm(tokens, norm_in)
    qkv_full, out_full, gate_up_all, down_all = (
        lax.all_gather(w_qkv, "dp", axis=0, tiled=True),
        lax.all_gather(w_out, "dp", axis=3, tiled=True),
        lax.all_gather(w_gate_up, "dp", axis=1, tiled=True),
        lax.all_gather(w_down, "dp", axis=2, tiled=True),
    )
    projected = jnp.dot(normed[0], qkv_full.reshape(width, -1), preferred_element_type=jnp.float32)[
        None
    ]
    projected = projected.reshape(1, tok_rows, kv_local, group_size + 2, head_dim)
    query_idx = lax.axis_index("ctx") * tok_rows + jnp.arange(tok_rows, dtype=jnp.int32)
    angles = rope_angles(query_idx.astype(jnp.float32), head_dim)
    queries = rotate(projected[:, :, :, :group_size, :], angles[None, :, None, None, :]).astype(
        jnp.bfloat16
    )
    keys_rot = rotate(projected[:, :, :, group_size, :], angles[None, :, None, :]).astype(
        jnp.bfloat16
    )
    values = projected[:, :, :, group_size + 1, :].astype(jnp.bfloat16)
    scale = 1.0 / math.sqrt(head_dim)
    last_query = lax.axis_index("ctx") * tok_rows + tok_rows - 1
    peak_init = jnp.full((1, kv_local, group_size, tok_rows), -1e30, jnp.float32)
    total_init = jnp.zeros((1, kv_local, group_size, tok_rows), jnp.float32)
    accum_init = jnp.zeros((1, kv_local, group_size, tok_rows, head_dim), jnp.float32)
    key_piece = lax.all_gather(keys_rot, "ctx", axis=1, tiled=True)
    value_piece = lax.all_gather(values, "ctx", axis=1, tiled=True)
    count = key_piece.shape[1]

    def compute(state):
        peak, totals, accum = state
        score_matrix = (
            jnp.einsum("bqkgd,bskd->bkgqs", queries, key_piece, preferred_element_type=jnp.float32)
            * scale
        )
        key_idx = jnp.arange(count, dtype=jnp.int32)
        causal = key_idx[None, :] <= query_idx[:, None]
        score_matrix = jnp.where(causal, score_matrix, -1e30)
        new_peak = jnp.maximum(peak, jnp.max(score_matrix, axis=-1))
        probs = jnp.where(causal, jnp.exp(score_matrix - new_peak[..., None]), 0.0)
        totals = jnp.sum(probs, axis=-1)
        update = jnp.einsum(
            "bkgqs,bskd->bkgqd",
            probs.astype(jnp.bfloat16),
            value_piece,
            preferred_element_type=jnp.float32,
        )
        accum = update
        return (new_peak, totals, accum)

    peak, totals, accum = lax.cond(
        jnp.int32(0) <= last_query,
        compute,
        lambda state: state,
        (peak_init, total_init, accum_init),
    )
    attended = jnp.transpose(accum / totals[..., None], (0, 3, 1, 2, 4)).astype(jnp.bfloat16)
    attended = attended.reshape(1, tok_rows, kv_local * group_size * head_dim)
    partial_sum = jnp.dot(
        attended[0], out_full.reshape(-1, width), preferred_element_type=jnp.float32
    )[None]
    head_total = lax.psum_scatter(
        partial_sum.astype(jnp.bfloat16), "exp", scatter_dimension=1, tiled=True
    ).astype(jnp.float32)
    rows = head_total.shape[1]
    own_tokens = lax.dynamic_slice_in_dim(tokens, lax.axis_index("exp") * rows, rows, 1)
    mixed = (own_tokens[0].astype(jnp.float32) + head_total[0]).astype(jnp.bfloat16)
    normed_mid = rms_norm(mixed, norm_mid)
    expert_count = w_router.shape[1]
    logits = jnp.dot(normed_mid, w_router, preferred_element_type=jnp.float32)
    choice_ids = expert_ids[0]
    picks = choice_ids[:, :, None] == jnp.arange(expert_count, dtype=jnp.int32)[None, None, :]
    chosen = jnp.sum(jnp.where(picks, logits[:, None, :], 0.0), axis=-1)
    gate_first = 1.0 / (1.0 + jnp.exp(chosen[:, 1] - chosen[:, 0]))
    gate_second = 1.0 - gate_first
    capacity = 6 * (rows // 16)
    exp_count = lax.axis_size("exp")
    exp_local = gate_up_all.shape[0]
    flat_index = choice_ids * capacity + slot_index[0]
    slot_cols = jnp.arange(expert_count * capacity, dtype=jnp.int32)
    placer = jnp.logical_or(
        slot_cols[:, None] == flat_index[None, :, 0], slot_cols[:, None] == flat_index[None, :, 1]
    ).astype(jnp.bfloat16)
    buffer_rows = jnp.dot(placer, normed_mid, preferred_element_type=jnp.float32).astype(
        jnp.bfloat16
    )
    buffer_rows = buffer_rows.reshape(exp_count, exp_local, capacity, width)
    received = lax.all_to_all(buffer_rows, "exp", split_axis=0, concat_axis=0, tiled=True)
    gathered_rows = lax.all_gather(received[None], "ctx", axis=0, tiled=True)
    gate_up_vals = jnp.einsum(
        "cnlrd,ldjf->cnlrjf", gathered_rows, gate_up_all, preferred_element_type=jnp.float32
    )
    hidden = (jax.nn.silu(gate_up_vals[..., 0, :]) * gate_up_vals[..., 1, :]).astype(jnp.bfloat16)
    summed_result = lax.psum_scatter(
        jnp.einsum("cnlrf,lfd->cnlrd", hidden, down_all, preferred_element_type=jnp.float32).astype(
            jnp.bfloat16
        ),
        "ctx",
        scatter_dimension=0,
        tiled=True,
    ).astype(jnp.float32)
    expert_out = summed_result[0].astype(jnp.bfloat16)
    returned = lax.all_to_all(expert_out, "exp", split_axis=0, concat_axis=0, tiled=True)
    returned = returned.reshape(expert_count * capacity, width)
    combiner = gate_first[:, None] * (flat_index[:, 0:1] == slot_cols[None, :]).astype(
        jnp.float32
    ) + gate_second[:, None] * (flat_index[:, 1:2] == slot_cols[None, :]).astype(jnp.float32)
    moe_total = jnp.dot(combiner, returned.astype(jnp.float32), precision=lax.Precision.HIGHEST)
    return (mixed.astype(jnp.float32) + moe_total).astype(jnp.bfloat16)[None]


def solution(mesh):
    placed = (
        P("dp", "ctx", None),
        P(),
        P("dp", "exp", None, None),
        P("exp", None, None, "dp"),
        P(),
        P(),
        P("exp", "dp", None, "ctx"),
        P("exp", "ctx", "dp"),
        P("dp", ("ctx", "exp"), None),
        P("dp", ("ctx", "exp"), None),
    )
    return jax.shard_map(
        on_device,
        mesh=mesh,
        in_specs=placed,
        out_specs=P("dp", ("ctx", "exp"), None),
        check_vma=False,
    )
```

profile of v0, /device:TPU:2, one launch (start us, length us, event | category | flops | bytes accessed | tf_op | source)
XLA Modules:
  0.0 595.8 jit_solution(7468417833645752006)
XLA Ops:
  6.5 0.0 copy-start
  6.5 0.0 all-gather.8.cloned.1.call-start
  6.5 4.8 copy.44
  11.3 0.0 copy-start.2
  11.3 0.0 copy-start.1
  11.3 0.0 all-gather.8.cloned.1.call-update
  11.3 0.0 all-gather.10.cloned.1.call-start
  11.4 0.7 all-gather.10.cloned.1.call-update
  12.1 0.0 reduce-scatter.3.cloned.1.call-start
  12.1 0.0 copy-done.2
  12.2 0.4 copy-done.1
  12.6 0.3 fusion.27
  12.8 0.2 multiply_cosine_fusion
  13.1 86.9 %all-gather.8.cloned.1.call-done = bf16[4096,1,6,128]{0,3,2,1:T(8,128)(2,1)} async-done(((bf16[2048,1,6,128]{0,3,2,1:T(8,128)(2,1)}), bf16[4096,1,6,128]{0,3,2,1:T(8,128)(2,1)}) %all-gather.8.cloned.1.call-update) | async-done | bytes 6291472 | tf_op jit(solution)/shard_map/all_gather | solution.py:47
  99.9 4.6 fusion.36
  104.6 0.2 fusion.54
  104.9 21.1 %all_gather.22 = bf16[1,2048,1,128]{1,3,2,0:T(8,128)(2,1)S(1)} all-gather(bf16[1,128,1,128]{1,3,2,0:T(8,128)(2,1)S(1)} %pad_maximum_fusion.1), channel_id=1, replica_groups=mesh['ctx'=16,'exp'=8,'dp'=2] {'ctx'}, dimensions={1}, use_global_device_ids=true | all-gather | bytes 557056 | tf_op jit(solution)/shard_map/all_gather | solution.py:70
  126.0 25.5 %all-gather = bf16[1,2048,1,1,128]{1,4,3,2,0:T(8,128)(2,1)S(1)} all-gather(bf16[1,128,1,1,128]{1,4,3,2,0:T(8,128)(2,1)S(1)} %slice.86), channel_id=2, replica_groups=mesh['ctx'=16,'exp'=8,'dp'=2] {'ctx'}, dimensions={1}, use_global_device_ids=true | all-gather | bytes 557056 | tf_op jit(solution)/shard_map/all_gather | solution.py:71
  151.4 3.1 conditional.1
  151.4 0.2 iota_compare_fusion
  151.6 0.8 fusion
  152.4 1.1 fusion.7
  153.5 1.0 fusion.2
  154.5 10.0 %all-gather.10.cloned.1.call-done = bf16[1,4,128,4096]{3,2,1,0:T(8,128)(2,1)} async-done(((bf16[1,4,128,2048]{3,2,1,0:T(8,128)(2,1)}), bf16[1,4,128,4096]{3,2,1,0:T(8,128)(2,1)}) %all-gather.10.cloned.1.call-update) | async-done | bytes 4194320 | tf_op jit(solution)/shard_map/all_gather | solution.py:48
  164.6 3.9 fusion.23
  168.5 0.0 reduce-scatter.3.cloned.1.call-update
  168.5 0.0 all-gather.12.cloned.1.call-start
  168.6 4.9 copy.51
  173.5 0.0 copy-start.3
  173.5 0.0 copy-start.4
  173.5 0.0 copy-start.5
  173.5 0.0 all-gather.12.cloned.1.call-update
  173.5 0.0 all-gather.16.cloned.1.call-start
  173.5 0.6 copy-done.3
  174.2 0.0 copy-done.4
  174.2 0.0 copy-done.5
  174.2 36.3 %reduce-scatter.3.cloned.1.call-done = bf16[1,16,4096]{2,1,0:T(8,128)(2,1)} async-done(((bf16[1,128,4096]{2,1,0:T(8,128)(2,1)}), bf16[1,16,4096]{2,1,0:T(8,128)(2,1)}) %reduce-scatter.3.cloned.1.call-update) | async-done | bytes 131088 | tf_op jit(solution)/shard_map/reduce_scatter | solution.py:106
  210.5 1.1 fusion.45
  211.6 0.3 convolution_convert_fusion.2
  211.9 0.1 reshape.364
  212.0 17.6 %all_to_all.10 = bf16[8,1,6,4096]{3,2,1,0:T(8,128)(2,1)S(1)} all-to-all(bf16[8,1,6,4096]{3,2,1,0:T(8,128)(2,1)S(1)} %bitcast.132), channel_id=1, replica_groups=mesh['ctx'=16,'exp'=8,'dp'=2] {'exp'}, dimensions={0} | all-to-all | bytes 786432 | tf_op jit(solution)/shard_map/all_to_all | solution.py:132
  229.6 1.0 copy.50
  230.6 0.0 all-gather.16.cloned.1.call-update
  230.6 0.0 all-gather.14.cloned.1.call-start
  230.7 0.5 all-gather.14.cloned.1.call-update
  231.2 0.2 reduce-scatter.5.cloned.1.call-start
  231.4 88.6 %all-gather.12.cloned.1.call-done = bf16[1,4096,2,512]{3,1,2,0:T(8,128)(2,1)} async-done(((bf16[1,2048,2,512]{3,1,2,0:T(8,128)(2,1)}), bf16[1,4096,2,512]{3,1,2,0:T(8,128)(2,1)}) %all-gather.12.cloned.1.call-update) | async-done | bytes 8388624 | tf_op jit(solution)/shard_map/all_gather | solution.py:49
  320.0 72.3 %all-gather.16.cloned.1.call-done = bf16[128,1,6,4096]{3,0,2,1:T(8,128)(2,1)} async-done(((bf16[8,1,6,4096]{3,0,2,1:T(8,128)(2,1)}), bf16[128,1,6,4096]{3,0,2,1:T(8,128)(2,1)}) %all-gather.16.cloned.1.call-update) | async-done | bytes 6291472 | tf_op jit(solution)/shard_map/all_gather | solution.py:133
  392.3 12.1 %fusion.30 = f32[16,8,1,6,2,512]{5,1,4,3,0,2:T(8,128)} fusion(bf16[1,4096,2,512]{3,1,2,0:T(8,128)(2,1)} %all-gather.12.cloned.1.call-done, bf16[128,1,6,4096]{3,0,2,1:T(8,128)(2,1)} %all-gather.16.cloned.1.call-done), kind=kOutput, calls=%fused_computation.38 | convolution fusion | flops 6442450944 | bytes 17825792 | tf_op jit(solution)/shard_map/cnlrd,ldjf->cnlrjf/dot_general | solution.py:134
  404.4 50.6 %all-gather.14.cloned.1.call-done = bf16[1,512,4096]{2,1,0:T(8,128)(2,1)} async-done(((bf16[1,512,2048]{2,1,0:T(8,128)(2,1)}), bf16[1,512,4096]{2,1,0:T(8,128)(2,1)}) %all-gather.14.cloned.1.call-update) | async-done | bytes 4194320 | tf_op jit(solution)/shard_map/all_gather | solution.py:50
  455.0 9.2 %fusion.22 = bf16[16,8,1,6,4096]{4,1,3,0,2:T(8,128)(2,1)} fusion(bf16[1,512,4096]{2,1,0:T(8,128)(2,1)} %all-gather.14.cloned.1.call-done, f32[16,8,1,6,2,512]{5,1,4,3,0,2:T(8,128)} %fusion.30), kind=kOutput, calls=%fused_computation.25 | convolution fusion | flops 3226730496 | bytes 13631488 | tf_op jit(solution)/shard_map/cnlrf,lfd->cnlrd/dot_general | solution.py:139
  464.2 0.0 reduce-scatter.5.cloned.1.call-update
  464.3 98.2 %reduce-scatter.5.cloned.1.call-done = bf16[1,8,1,6,4096]{4,1,3,0,2:T(8,128)(2,1)} async-done(((bf16[16,8,1,6,4096]{4,1,3,0,2:T(8,128)(2,1)}), bf16[1,8,1,6,4096]{4,1,3,0,2:T(8,128)(2,1)}) %reduce-scatter.5.cloned.1.call-update) | async-done | bytes 393232 | tf_op jit(solution)/shard_map/reduce_scatter | solution.py:138
  562.5 2.0 copy.53
  564.5 7.0 %all-to-all-start.1 = ((bf16[8,1,6,4096]{3,2,1,0:T(8,128)(2,1)}), bf16[8,1,6,4096]{3,2,1,0:T(8,128)(2,1)S(1)}, u32[]{:S(2)}, u32[]{:S(2)}) async-start(bf16[8,1,6,4096]{3,2,1,0:T(8,128)(2,1)} %copy.53), calls=%async_computation.3 | async-start | bytes 1048576 | tf_op jit(solution)/shard_map/all_to_all | solution.py:147
  571.5 0.0 copy-done
  571.5 0.2 fusion.58
  571.8 16.1 %all-to-all-done.1 = bf16[8,1,6,4096]{3,2,1,0:T(8,128)(2,1)S(1)} async-done(((bf16[8,1,6,4096]{3,2,1,0:T(8,128)(2,1)}), bf16[8,1,6,4096]{3,2,1,0:T(8,128)(2,1)S(1)}, u32[]{:S(2)}, u32[]{:S(2)}) %all-to-all-start.1) | async-done | bytes 393248 | tf_op jit(solution)/shard_map/all_to_all | solution.py:147
  587.8 0.1 reshape.368
  588.0 1.0 fusion.25
  (19 shorter events, 0.2 us)
Async XLA Ops:
  6.5 565.0 %copy-start = (bf16[4096,8]{0,1:T(8,128)(2,1)S(1)}, bf16[4096,8]{0,1:T(8,128)(2,1)}, u32[]{:S(2)}) copy-start(bf16[4096,8]{0,1:T(8,128)(2,1)} %param.17) | copy-start | bytes 196612
  6.5 93.4 %all-gather.8.cloned.1.call-start = ((), (), s32[]{:S(2)}) async-start(), calls=%async_computation.4 | async-start | bytes 9437184 | tf_op jit(solution)/shard_map/all_gather | solution.py:47
  11.3 0.8 copy-start.2
  11.3 1.2 copy-start.1
  11.3 153.2 %all-gather.10.cloned.1.call-start = ((), (), s32[]{:S(2)}) async-start(), calls=%async_computation.5 | async-start | bytes 6291456 | tf_op jit(solution)/shard_map/all_gather | solution.py:48
  12.1 198.4 %reduce-scatter.3.cloned.1.call-start = ((), (), s32[]{:S(2)}) async-start(), calls=%async_computation.6 | async-start | bytes 1179648 | tf_op jit(solution)/shard_map/reduce_scatter | solution.py:106
  168.5 151.5 %all-gather.12.cloned.1.call-start = ((), (), s32[]{:S(2)}) async-start(), calls=%async_computation.7 | async-start | bytes 12582912 | tf_op jit(solution)/shard_map/all_gather | solution.py:49
  173.5 0.7 copy-start.3
  173.5 0.7 copy-start.4
  173.5 0.7 copy-start.5
  173.5 218.9 %all-gather.16.cloned.1.call-start = ((), (), s32[]{:S(2)}) async-start(), calls=%async_computation.10 | async-start | bytes 6684672 | tf_op jit(solution)/shard_map/all_gather | solution.py:133
  230.6 224.4 %all-gather.14.cloned.1.call-start = ((), (), s32[]{:S(2)}) async-start(), calls=%async_computation.8 | async-start | bytes 6291456 | tf_op jit(solution)/shard_map/all_gather | solution.py:50
  231.2 331.3 %reduce-scatter.5.cloned.1.call-start = ((), (), s32[]{:S(2)}) async-start(), calls=%async_computation.9 | async-start | bytes 6684672 | tf_op jit(solution)/shard_map/reduce_scatter | solution.py:138
  564.5 23.4 %all-to-all-start.1 = ((bf16[8,1,6,4096]{3,2,1,0:T(8,128)(2,1)}), bf16[8,1,6,4096]{3,2,1,0:T(8,128)(2,1)S(1)}, u32[]{:S(2)}, u32[]{:S(2)}) async-start(bf16[8,1,6,4096]{3,2,1,0:T(8,128)(2,1)} %copy.53), calls=%async_computation.3 | async-start | bytes 1048576 | tf_op jit(solution)/shard_map/all_to_all | solution.py:147
Sparse Core Ops, SparseCore 0:
  11.5 88.4 all-gather.7
  101.7 62.8 all-gather.9
  168.6 41.8 reduce-scatter.2
  212.2 107.8 all-gather.11
  322.7 69.6 all-gather.15
  394.0 60.9 all-gather.13
  464.4 98.0 reduce-scatter.4
where the time goes:
time: 596 us
  waiting for transfers between devices  460 us (77%)
  blocking collectives  64.1 us (11%)
  matrix products  33.3 us (6%)
  local copies, waits for them, and re-layouts  14 us (2%)
  between operations  13.7 us (2%)
  starting transfers between devices  7.44 us (1%)
    reduce_scatter x1, waiting for transfers between devices, on_device(): lax.psum_scatter(jnp.einsum('cnlrf,lfd->cnlrd', hidden, down_all, preferr...  98.2 us
    all_gather x1, waiting for transfers between devices, on_device(): lax.all_gather(w_gate_up, 'dp', axis=1, tiled=True)  88.6 us
    all_gather x1, waiting for transfers between devices, on_device(): lax.all_gather(w_qkv, 'dp', axis=0, tiled=True)  86.9 us
    all_gather x1, waiting for transfers between devices, on_device(): gathered_rows = lax.all_gather(received[None], 'ctx', axis=0, tiled=True)  72.3 us
    all_gather x1, waiting for transfers between devices, on_device(): lax.all_gather(w_down, 'dp', axis=2, tiled=True)  50.6 us
    reduce_scatter x1, waiting for transfers between devices, on_device(): lax.psum_scatter(partial_sum.astype(jnp.bfloat16), 'exp', scatter_dimensi...  36.3 us
    all_gather x1, blocking collectives, on_device(): value_piece = lax.all_gather(values, 'ctx', axis=1, tiled=True)  25.5 us
    all_gather x1, blocking collectives, on_device(): key_piece = lax.all_gather(keys_rot, 'ctx', axis=1, tiled=True)  21.1 us
  transfers between devices with their start and end apart: 8, of which 8 were waited for; matrix products, arithmetic and copies ran while one was open for 5% of the time, Pallas kernels for 0%

commit v1 on v0

--- a/solution.py
+++ b/solution.py
@@ -6,6 +6,18 @@
 
 EPSILON = 1e-05
 ROPE_BASE = 1000000.0
+
+
+def split_up(x, dim, count):
+    lengths = x.shape
+    tiles = x.reshape(*lengths[:dim], count, lengths[dim] // count, *lengths[dim + 1 :])
+    return jnp.moveaxis(tiles, dim, 0)
+
+
+def laid_out(tiles, dim):
+    dims = list(tiles.shape[1:])
+    dims[dim] *= tiles.shape[0]
+    return jnp.moveaxis(tiles, 0, dim).reshape(dims)
 
 
 def rms_norm(values, gain):
@@ -129,7 +141,14 @@
         jnp.bfloat16
     )
     buffer_rows = buffer_rows.reshape(exp_count, exp_local, capacity, width)
-    received = lax.all_to_all(buffer_rows, "exp", split_axis=0, concat_axis=0, tiled=True)
+    size, here = (lax.axis_size("exp"), lax.axis_index("exp"))
+    blocks = split_up(buffer_rows, 0, size)
+    outs = [blocks[here]]
+    for lap in range(1, size):
+        sent = blocks[here ^ lap]
+        outs.append(lax.ppermute(sent, "exp", [(i, i ^ lap) for i in range(size)]))
+    blocks = jnp.stack(outs)[here ^ jnp.arange(size)]
+    received = laid_out(blocks, 0)
     gathered_rows = lax.all_gather(received[None], "ctx", axis=0, tiled=True)
     gate_up_vals = jnp.einsum(
         "cnlrd,ldjf->cnlrjf", gathered_rows, gate_up_all, preferred_element_type=jnp.float32

time: 596 us -> 596 us (level)
  blocking collectives: 64.1 us -> 46.6 us
  starting transfers between devices: 7.44 us -> 21.2 us
    all_to_all x1 -> x0, blocking collectives: 17.6 us -> none  [on_device(): lax.all_to_all(buffer_rows, 'exp', split_axis=0, concat_axis=0, tiled=True)]
    ppermute x0 -> x7, starting transfers between devices: none -> 13.9 us  [on_device(): outs.append(lax.ppermute(sent, 'exp', [(i, i ^ lap) for i in range(size)]))]
  transfers between devices with their start and end apart: 8 -> 15, of which waited for: 8 -> 11; matrix products, arithmetic and copies ran while one was open for 5% -> 5% of each run, Pallas kernels for 0% -> 0%
where the time goes in v1:
time: 596 us
  waiting for transfers between devices  463 us (78%)
  blocking collectives  46.6 us (8%)
  matrix products  33.3 us (6%)
  starting transfers between devices  21.2 us (4%)
  local copies, waits for them, and re-layouts  14.6 us (2%)
  between operations  13.7 us (2%)
    reduce_scatter x1, waiting for transfers between devices, on_device(): lax.psum_scatter(jnp.einsum('cnlrf,lfd->cnlrd', hidden, down_all, preferr...  98.2 us
    all_gather x1, waiting for transfers between devices, on_device(): lax.all_gather(w_gate_up, 'dp', axis=1, tiled=True)  87.5 us
    all_gather x1, waiting for transfers between devices, on_device(): lax.all_gather(w_qkv, 'dp', axis=0, tiled=True)  86.9 us
    all_gather x1, waiting for transfers between devices, on_device(): gathered_rows = lax.all_gather(received[None], 'ctx', axis=0, tiled=True)  72.3 us
    all_gather x1, waiting for transfers between devices, on_device(): lax.all_gather(w_down, 'dp', axis=2, tiled=True)  50.6 us
    reduce_scatter x1, waiting for transfers between devices, on_device(): lax.psum_scatter(partial_sum.astype(jnp.bfloat16), 'exp', scatter_dimensi...  36.3 us
    all_gather x1, blocking collectives, on_device(): value_piece = lax.all_gather(values, 'ctx', axis=1, tiled=True)  25.5 us
    all_gather x1, blocking collectives, on_device(): key_piece = lax.all_gather(keys_rot, 'ctx', axis=1, tiled=True)  21.1 us
  transfers between devices with their start and end apart: 15, of which 11 were waited for; matrix products, arithmetic and copies ran while one was open for 5% of the time, Pallas kernels for 0%

profile of v1, /device:TPU:2, one launch (start us, length us, event | category | flops | bytes accessed | tf_op | source)
XLA Modules:
  0.0 595.8 jit_solution(13335160625815674971)
XLA Ops:
  6.5 4.8 copy.43
  11.3 0.0 all-gather.8.cloned.1.call-update
  11.3 0.0 all-gather.10.cloned.1.call-start
  11.4 0.7 all-gather.10.cloned.1.call-update
  12.1 0.0 reduce-scatter.3.cloned.1.call-start
  12.2 0.4 copy-done.1
  12.6 0.3 fusion.27
  12.8 0.2 multiply_cosine_fusion
  13.1 86.9 %all-gather.8.cloned.1.call-done = bf16[4096,1,6,128]{0,3,2,1:T(8,128)(2,1)} async-done(((bf16[2048,1,6,128]{0,3,2,1:T(8,128)(2,1)}), bf16[4096,1,6,128]{0,3,2,1:T(8,128)(2,1)}) %all-gather.8.cloned.1.call-update) | async-done | bytes 6291472 | tf_op jit(solution)/shard_map/all_gather | solution.py:59
  99.9 4.6 fusion.36
  104.6 0.2 fusion.54
  104.9 21.1 %all_gather.22 = bf16[1,2048,1,128]{1,3,2,0:T(8,128)(2,1)S(1)} all-gather(bf16[1,128,1,128]{1,3,2,0:T(8,128)(2,1)S(1)} %pad_maximum_fusion.1), channel_id=1, replica_groups=mesh['ctx'=16,'exp'=8,'dp'=2] {'ctx'}, dimensions={1}, use_global_device_ids=true | all-gather | bytes 557056 | tf_op jit(solution)/shard_map/all_gather | solution.py:82
  125.9 25.5 %all-gather = bf16[1,2048,1,1,128]{1,4,3,2,0:T(8,128)(2,1)S(1)} all-gather(bf16[1,128,1,1,128]{1,4,3,2,0:T(8,128)(2,1)S(1)} %slice.88), channel_id=2, replica_groups=mesh['ctx'=16,'exp'=8,'dp'=2] {'ctx'}, dimensions={1}, use_global_device_ids=true | all-gather | bytes 557056 | tf_op jit(solution)/shard_map/all_gather | solution.py:83
  151.4 3.1 conditional.1
  151.4 0.2 iota_compare_fusion
  151.6 0.8 fusion
  152.4 1.0 fusion.7
  153.5 1.0 fusion.2
  154.5 10.0 %all-gather.10.cloned.1.call-done = bf16[1,4,128,4096]{3,2,1,0:T(8,128)(2,1)} async-done(((bf16[1,4,128,2048]{3,2,1,0:T(8,128)(2,1)}), bf16[1,4,128,4096]{3,2,1,0:T(8,128)(2,1)}) %all-gather.10.cloned.1.call-update) | async-done | bytes 4194320 | tf_op jit(solution)/shard_map/all_gather | solution.py:60
  164.6 3.9 fusion.23
  168.5 0.0 reduce-scatter.3.cloned.1.call-update
  168.5 0.0 all-gather.12.cloned.1.call-start
  168.6 4.9 copy.49
  173.5 0.0 all-gather.12.cloned.1.call-update
  173.5 0.0 all-gather.16.cloned.1.call-start
  173.6 0.6 copy-done.3
  174.2 36.3 %reduce-scatter.3.cloned.1.call-done = bf16[1,16,4096]{2,1,0:T(8,128)(2,1)} async-done(((bf16[1,128,4096]{2,1,0:T(8,128)(2,1)}), bf16[1,16,4096]{2,1,0:T(8,128)(2,1)}) %reduce-scatter.3.cloned.1.call-update) | async-done | bytes 131088 | tf_op jit(solution)/shard_map/reduce_scatter | solution.py:118
  210.5 1.1 fusion.45
  211.6 0.3 convolution_convert_fusion.2
  211.9 0.1 reshape_reshape.3
  212.0 0.1 dynamic-slice_bitcast_fusion
  212.1 1.0 collective-permute-start
  213.1 2.6 collective-permute-start.1
  215.7 0.9 collective-permute-start.2
  216.6 3.2 collective-permute-start.3
  219.8 1.2 collective-permute-start.4
  221.0 0.0 collective-permute-done
  221.0 2.8 collective-permute-start.5
  223.9 0.0 collective-permute-done.1
  223.9 2.1 collective-permute-start.6
  226.0 0.0 collective-permute-done.2
  226.1 0.0 collective-permute-done.3
  226.1 1.3 collective-permute-done.4
  227.4 0.6 collective-permute-done.5
  228.0 2.3 collective-permute-done.6
  230.3 0.6 gather_fusion
  230.9 1.0 copy.48
  231.9 0.0 all-gather.16.cloned.1.call-update
  231.9 0.0 all-gather.14.cloned.1.call-start
  232.0 0.5 all-gather.14.cloned.1.call-update
  232.5 0.0 reduce-scatter.5.cloned.1.call-start
  232.6 87.5 %all-gather.12.cloned.1.call-done = bf16[1,4096,2,512]{3,1,2,0:T(8,128)(2,1)} async-done(((bf16[1,2048,2,512]{3,1,2,0:T(8,128)(2,1)}), bf16[1,4096,2,512]{3,1,2,0:T(8,128)(2,1)}) %all-gather.12.cloned.1.call-update) | async-done | bytes 8388624 | tf_op jit(solution)/shard_map/all_gather | solution.py:61
  320.0 72.3 %all-gather.16.cloned.1.call-done = bf16[128,6,4096]{2,0,1:T(8,128)(2,1)} async-done(((bf16[8,6,4096]{2,0,1:T(8,128)(2,1)}), bf16[128,6,4096]{2,0,1:T(8,128)(2,1)}) %all-gather.16.cloned.1.call-update) | async-done | bytes 6291472 | tf_op jit(solution)/shard_map/all_gather | solution.py:152
  392.3 12.1 %fusion.30 = f32[16,8,1,6,2,512]{5,1,4,3,0,2:T(8,128)} fusion(bf16[1,4096,2,512]{3,1,2,0:T(8,128)(2,1)} %all-gather.12.cloned.1.call-done, bf16[128,6,4096]{2,0,1:T(8,128)(2,1)} %all-gather.16.cloned.1.call-done), kind=kOutput, calls=%fused_computation.39 | convolution fusion | flops 6442450944 | bytes 17825792 | tf_op jit(solution)/shard_map/cnlrd,ldjf->cnlrjf/dot_general | solution.py:153
  404.4 50.6 %all-gather.14.cloned.1.call-done = bf16[1,512,4096]{2,1,0:T(8,128)(2,1)} async-done(((bf16[1,512,2048]{2,1,0:T(8,128)(2,1)}), bf16[1,512,4096]{2,1,0:T(8,128)(2,1)}) %all-gather.14.cloned.1.call-update) | async-done | bytes 4194320 | tf_op jit(solution)/shard_map/all_gather | solution.py:62
  455.0 9.2 %fusion.22 = bf16[16,8,1,6,4096]{4,1,3,0,2:T(8,128)(2,1)} fusion(bf16[1,512,4096]{2,1,0:T(8,128)(2,1)} %all-gather.14.cloned.1.call-done, f32[16,8,1,6,2,512]{5,1,4,3,0,2:T(8,128)} %fusion.30), kind=kOutput, calls=%fused_computation.26 | convolution fusion | flops 3226730496 | bytes 13631488 | tf_op jit(solution)/shard_map/cnlrf,lfd->cnlrd/dot_general | solution.py:158
  464.2 0.0 reduce-scatter.5.cloned.1.call-update
  464.2 98.2 %reduce-scatter.5.cloned.1.call-done = bf16[1,8,1,6,4096]{4,1,3,0,2:T(8,128)(2,1)} async-done(((bf16[16,8,1,6,4096]{4,1,3,0,2:T(8,128)(2,1)}), bf16[1,8,1,6,4096]{4,1,3,0,2:T(8,128)(2,1)}) %reduce-scatter.5.cloned.1.call-update) | async-done | bytes 393232 | tf_op jit(solution)/shard_map/reduce_scatter | solution.py:157
  562.4 2.0 copy.51
  564.5 7.0 %all-to-all-start = ((bf16[8,1,6,4096]{3,2,1,0:T(8,128)(2,1)}), bf16[8,1,6,4096]{3,2,1,0:T(8,128)(2,1)S(1)}, u32[]{:S(2)}, u32[]{:S(2)}) async-start(bf16[8,1,6,4096]{3,2,1,0:T(8,128)(2,1)} %copy.51), calls=%async_computation.2 | async-start | bytes 1048576 | tf_op jit(solution)/shard_map/all_to_all | solution.py:166
  571.5 0.2 fusion.58
  571.7 16.1 %all-to-all-done = bf16[8,1,6,4096]{3,2,1,0:T(8,128)(2,1)S(1)} async-done(((bf16[8,1,6,4096]{3,2,1,0:T(8,128)(2,1)}), bf16[8,1,6,4096]{3,2,1,0:T(8,128)(2,1)S(1)}, u32[]{:S(2)}, u32[]{:S(2)}) %all-to-all-start) | async-done | bytes 393248 | tf_op jit(solution)/shard_map/all_to_all | solution.py:166
  587.8 0.1 reshape.380
  588.0 1.0 fusion.25
  (39 shorter events, 0.3 us)
Async XLA Ops:
  6.5 564.9 %copy-start = (bf16[4096,8]{0,1:T(8,128)(2,1)S(1)}, bf16[4096,8]{0,1:T(8,128)(2,1)}, u32[]{:S(2)}) copy-start(bf16[4096,8]{0,1:T(8,128)(2,1)} %param.17) | copy-start | bytes 196612
  6.5 93.4 %all-gather.8.cloned.1.call-start = ((), (), s32[]{:S(2)}) async-start(), calls=%async_computation.3 | async-start | bytes 9437184 | tf_op jit(solution)/shard_map/all_gather | solution.py:59
  11.3 0.8 copy-start.2
  11.3 1.2 copy-start.1
  11.3 153.2 %all-gather.10.cloned.1.call-start = ((), (), s32[]{:S(2)}) async-start(), calls=%async_computation.4 | async-start | bytes 6291456 | tf_op jit(solution)/shard_map/all_gather | solution.py:60
  12.1 198.4 %reduce-scatter.3.cloned.1.call-start = ((), (), s32[]{:S(2)}) async-start(), calls=%async_computation.5 | async-start | bytes 1179648 | tf_op jit(solution)/shard_map/reduce_scatter | solution.py:118
  168.5 151.5 %all-gather.12.cloned.1.call-start = ((), (), s32[]{:S(2)}) async-start(), calls=%async_computation.6 | async-start | bytes 12582912 | tf_op jit(solution)/shard_map/all_gather | solution.py:61
  173.5 0.7 copy-start.3
  173.5 0.7 copy-start.4
  173.5 0.7 copy-start.5
  173.5 218.8 %all-gather.16.cloned.1.call-start = ((), (), s32[]{:S(2)}) async-start(), calls=%async_computation.9 | async-start | bytes 6684672 | tf_op jit(solution)/shard_map/all_gather | solution.py:152
  212.1 8.9 %collective-permute-start = (bf16[1,1,6,4096]{3,2,1,0:T(8,128)(2,1)S(1)}, bf16[1,1,6,4096]{3,2,1,0:T(8,128)(2,1)S(1)}, u32[]{:S(2)}, u32[]{:S(2)}) collective-permute-start(bf16[1,1,6,4096]{3,2,1,0:T(8,128)(2,1)S(1)} %get-tuple-element.59), channel_id=1, source_target_pairs={{0,2},{2,0},{4,6},{6,4},{8,10},{10,8},{12,14},{14,12},{1,3},{3,1},... | collective-permute-start | bytes 147464 | tf_op jit(solution)/shard_map/ppermute | solution.py:149
  213.1 10.8 %collective-permute-start.1 = (bf16[1,1,6,4096]{3,2,1,0:T(8,128)(2,1)S(1)}, bf16[1,1,6,4096]{3,2,1,0:T(8,128)(2,1)S(1)}, u32[]{:S(2)}, u32[]{:S(2)}) collective-permute-start(bf16[1,1,6,4096]{3,2,1,0:T(8,128)(2,1)S(1)} %get-tuple-element.58), channel_id=1, source_target_pairs={{0,4},{2,6},{4,0},{6,2},{8,12},{10,14},{12,8},{14,10},{1,5},{3,7},... | collective-permute-start | bytes 147464 | tf_op jit(solution)/shard_map/ppermute | solution.py:149
  215.7 10.3 %collective-permute-start.2 = (bf16[1,1,6,4096]{3,2,1,0:T(8,128)(2,1)S(1)}, bf16[1,1,6,4096]{3,2,1,0:T(8,128)(2,1)S(1)}, u32[]{:S(2)}, u32[]{:S(2)}) collective-permute-start(bf16[1,1,6,4096]{3,2,1,0:T(8,128)(2,1)S(1)} %get-tuple-element.57), channel_id=1, source_target_pairs={{0,6},{2,4},{4,2},{6,0},{8,14},{10,12},{12,10},{14,8},{1,7},{3,5},... | collective-permute-start | bytes 147464 | tf_op jit(solution)/shard_map/ppermute | solution.py:149
  216.6 9.5 %collective-permute-start.3 = (bf16[1,1,6,4096]{3,2,1,0:T(8,128)(2,1)S(1)}, bf16[1,1,6,4096]{3,2,1,0:T(8,128)(2,1)S(1)}, u32[]{:S(2)}, u32[]{:S(2)}) collective-permute-start(bf16[1,1,6,4096]{3,2,1,0:T(8,128)(2,1)S(1)} %get-tuple-element.56), channel_id=1, source_target_pairs={{0,8},{2,10},{4,12},{6,14},{8,0},{10,2},{12,4},{14,6},{1,9},{3,11}... | collective-permute-start | bytes 147464 | tf_op jit(solution)/shard_map/ppermute | solution.py:149
  219.8 7.6 %collective-permute-start.4 = (bf16[1,1,6,4096]{3,2,1,0:T(8,128)(2,1)S(1)}, bf16[1,1,6,4096]{3,2,1,0:T(8,128)(2,1)S(1)}, u32[]{:S(2)}, u32[]{:S(2)}) collective-permute-start(bf16[1,1,6,4096]{3,2,1,0:T(8,128)(2,1)S(1)} %get-tuple-element.55), channel_id=1, source_target_pairs={{0,10},{2,8},{4,14},{6,12},{8,2},{10,0},{12,6},{14,4},{1,11},{3,9}... | collective-permute-start | bytes 147464 | tf_op jit(solution)/shard_map/ppermute | solution.py:149
  221.0 7.0 %collective-permute-start.5 = (bf16[1,1,6,4096]{3,2,1,0:T(8,128)(2,1)S(1)}, bf16[1,1,6,4096]{3,2,1,0:T(8,128)(2,1)S(1)}, u32[]{:S(2)}, u32[]{:S(2)}) collective-permute-start(bf16[1,1,6,4096]{3,2,1,0:T(8,128)(2,1)S(1)} %get-tuple-element.54), channel_id=1, source_target_pairs={{0,12},{2,14},{4,8},{6,10},{8,4},{10,6},{12,0},{14,2},{1,13},{3,15... | collective-permute-start | bytes 147464 | tf_op jit(solution)/shard_map/ppermute | solution.py:149
  223.9 6.4 %collective-permute-start.6 = (bf16[1,1,6,4096]{3,2,1,0:T(8,128)(2,1)S(1)}, bf16[1,1,6,4096]{3,2,1,0:T(8,128)(2,1)S(1)}, u32[]{:S(2)}, u32[]{:S(2)}) collective-permute-start(bf16[1,1,6,4096]{3,2,1,0:T(8,128)(2,1)S(1)} %get-tuple-element.53), channel_id=1, source_target_pairs={{0,14},{2,12},{4,10},{6,8},{8,6},{10,4},{12,2},{14,0},{1,15},{3,13... | collective-permute-start | bytes 147464 | tf_op jit(solution)/shard_map/ppermute | solution.py:149
  231.9 223.0 %all-gather.14.cloned.1.call-start = ((), (), s32[]{:S(2)}) async-start(), calls=%async_computation.7 | async-start | bytes 6291456 | tf_op jit(solution)/shard_map/all_gather | solution.py:62
  232.5 329.9 %reduce-scatter.5.cloned.1.call-start = ((), (), s32[]{:S(2)}) async-start(), calls=%async_computation.8 | async-start | bytes 6684672 | tf_op jit(solution)/shard_map/reduce_scatter | solution.py:157
  564.5 23.4 %all-to-all-start = ((bf16[8,1,6,4096]{3,2,1,0:T(8,128)(2,1)}), bf16[8,1,6,4096]{3,2,1,0:T(8,128)(2,1)S(1)}, u32[]{:S(2)}, u32[]{:S(2)}) async-start(bf16[8,1,6,4096]{3,2,1,0:T(8,128)(2,1)} %copy.51), calls=%async_computation.2 | async-start | bytes 1048576 | tf_op jit(solution)/shard_map/all_to_all | solution.py:166
Sparse Core Ops, SparseCore 0:
  11.5 88.4 all-gather.7
  101.7 62.8 all-gather.9
  168.6 41.7 reduce-scatter.2
  212.1 107.8 all-gather.11
  322.6 69.6 all-gather.15
  394.0 60.9 all-gather.13
  464.4 98.0 reduce-scatter.4
